TPU v7x, 32 devices: a whole 2x2x4 slice. The times are simulated.
32 devices in a mesh: depth: 4 (over y, x), lat: 8 (over z, core).
Axes of the slice: x: 2, y: 2, z: 4, core: 2. Of those that a mesh axis runs over, the one named last changes fastest.
Arguments:
- probe: bfloat16 [2, 256, 256], replicated, may hold values from -6 to 6
- positions: int32 [2, 32, 2], P(None, 'lat'), may hold values from 0 to 255
- object_phase: bfloat16 [4, 2048, 512], P('depth', 'lat'), may hold values from -3.140625 to 3.140625
- propagator: float32 [256, 256], replicated, may hold values from -3.140625 to 3.140625
- stored: bfloat16 [4, 32, 2, 256, 256], P('depth', 'lat'), may hold values from -6 to 6
- measured: float32 [32, 256, 256], P('lat'), may hold values from 0 to 2
Outputs:
- leaving: bfloat16 [4, 32, 2, 256, 256], P('depth', 'lat')
- gradient: float32 [4, 2, 2048, 512], P('depth', None, 'lat')
Inputs may be any that keep to these rules, and one draw needn't show every extreme that they name: positions[d, q, 0] and positions[d, q, 1] are the row and column of the corner of probe q's window inside the tile of probe q; windows reach into the next tile's first rows.
All inputs are finite; a program needn't handle non-finite values.
Results may differ from a plain program's by a relative error of at most 0.04.
Values may be sent and summed in bfloat16 or wider, within the bound.
A program may use at most 64 MiB of HBM per device.

v0:
```python
import math

import jax
import jax.numpy as jnp
from jax import lax
from jax.sharding import PartitionSpec as P


def from_behind(x, axis, by):
    devices = lax.axis_size(axis)
    return lax.ppermute(x, axis, [(i, (i + by) % devices) for i in range(devices)])


def shifted_2(block, axis, distance):
    devices = range(lax.axis_size(axis))
    route = [(i - distance, i) for i in devices if i - distance in devices]
    return lax.ppermute(block, axis, route)


def tables(npix):
    counter = jnp.arange(npix, dtype=jnp.int32)
    product = counter[:, None] * counter[None, :] % npix
    angles = 2.0 * math.pi / npix * product.astype(jnp.float32)
    factor = 1.0 / math.sqrt(npix)
    real_part = jnp.cos(angles) * factor
    imag_part = -jnp.sin(angles) * factor
    forward = jnp.stack(
        [jnp.stack([real_part, -imag_part]), jnp.stack([imag_part, real_part])]
    ).astype(jnp.bfloat16)
    inverse = jnp.stack(
        [jnp.stack([real_part, imag_part]), jnp.stack([-imag_part, real_part])]
    ).astype(jnp.bfloat16)
    return (forward, inverse)


def transform(table, wave):
    left = jnp.einsum("abjk,bkl->ajl", table, wave, preferred_element_type=jnp.float32).astype(
        jnp.bfloat16
    )
    return jnp.einsum("bjk,abkl->ajl", left, table, preferred_element_type=jnp.float32)


def times(first, second):
    first = first.astype(jnp.float32)
    real_part = first[0] * second[0] - first[1] * second[1]
    imag_part = first[0] * second[1] + first[1] * second[0]
    return jnp.stack([real_part, imag_part])


def conj_times(first, second):
    first = first.astype(jnp.float32)
    real_part = first[0] * second[0] + first[1] * second[1]
    imag_part = first[0] * second[1] - first[1] * second[0]
    return jnp.stack([real_part, imag_part])


def slice_forward(wave, transmit, kernel, forward, inverse):
    exited = times(wave, transmit).astype(jnp.bfloat16)
    spectrum = transform(forward, exited)
    shifted = times(kernel, spectrum).astype(jnp.bfloat16)
    return transform(inverse, shifted).astype(jnp.bfloat16)


def slice_adjoint(adjoint, wave, transmit, kernel, forward, inverse):
    spectrum = transform(forward, adjoint)
    shifted = conj_times(kernel, spectrum).astype(jnp.bfloat16)
    exited = transform(inverse, shifted)
    term = conj_times(wave, exited)
    return (conj_times(transmit, exited).astype(jnp.bfloat16), term)


def far_adjoint(exit_wave, intensity, forward, inverse):
    field = transform(forward, exit_wave)
    power = field[0] * field[0] + field[1] * field[1]
    weight = (power - intensity)[None] * field
    return transform(inverse, weight.astype(jnp.bfloat16)).astype(jnp.bfloat16)


def body(probe, positions, object_phase, propagator, stored, measured):
    npix = probe.shape[-1]
    slices, tile_rows, columns = object_phase.shape
    probes = positions.shape[1]
    depth_size = lax.axis_size("depth")
    segment = lax.axis_index("depth")
    forward, inverse = tables(npix)
    kernel = jnp.stack([jnp.cos(propagator), jnp.sin(propagator)])
    edge = from_behind(object_phase, "lat", -1)
    extended = jnp.concatenate([object_phase, edge], axis=1).astype(jnp.float32)
    transmit = jnp.stack([jnp.cos(extended), jnp.sin(extended)], axis=1)
    empty_wave = jnp.zeros((2, npix, npix), jnp.bfloat16)
    blank_piece = jnp.zeros((slices, 2, npix, npix), jnp.float32)

    def cut(row, col):
        return lax.dynamic_slice(transmit, (0, 0, row, col), (slices, 2, npix, npix))

    def advance(moment, carry):
        ahead_in, behind_in, leaving, gradient = carry
        ahead_index = moment - segment
        ahead_live = (ahead_index >= 0) & (ahead_index < probes)
        ahead_slot = jnp.clip(ahead_index, 0, probes - 1)
        ahead_row = positions[0, ahead_slot, 0]
        ahead_col = positions[0, ahead_slot, 1]
        entering = jnp.where(segment == 0, probe, ahead_in)

        def run_ahead():
            window = cut(ahead_row, ahead_col)
            wave = entering
            wave = slice_forward(wave, window[0], kernel, forward, inverse)
            return wave

        ahead_out = lax.cond(ahead_live, run_ahead, lambda: empty_wave)
        kept = jnp.where(ahead_live, ahead_out, leaving[ahead_slot])
        leaving = lax.dynamic_update_index_in_dim(leaving, kept, ahead_slot, 0)
        behind_index = moment - (depth_size - 1 - segment)
        behind_live = (behind_index >= 0) & (behind_index < probes)
        behind_slot = jnp.clip(behind_index, 0, probes - 1)
        behind_row = positions[1, behind_slot, 0]
        behind_col = positions[1, behind_slot, 1]

        def run_behind():
            window = cut(behind_row, behind_col)
            wave = stored[0, behind_slot]
            index = 0
            inputs = [wave]
            wave = slice_forward(wave, window[index], kernel, forward, inverse)
            final_wave = wave
            adjoint = lax.cond(
                segment == depth_size - 1,
                lambda: far_adjoint(final_wave, measured[behind_slot], forward, inverse),
                lambda: behind_in,
            )
            terms = [None] * slices
            for index in reversed(range(slices)):
                adjoint, terms[index] = slice_adjoint(
                    adjoint, inputs[index], window[index], kernel, forward, inverse
                )
            corner = (0, 0, behind_row, behind_col)
            summed = lax.dynamic_slice(gradient, corner, blank_piece.shape) + jnp.stack(terms)
            return (adjoint, lax.dynamic_update_slice(gradient, summed, corner))

        behind_out, gradient = lax.cond(behind_live, run_behind, lambda: (empty_wave, gradient))
        ahead_next = shifted_2(ahead_out, "depth", 1)
        behind_next = shifted_2(behind_out, "depth", -1)
        return (ahead_next, behind_next, leaving, gradient)

    ticks = probes + depth_size - 1
    initial = (
        empty_wave,
        empty_wave,
        jnp.zeros((probes, 2, npix, npix), jnp.bfloat16),
        jnp.zeros((slices, 2, tile_rows + npix, columns), jnp.float32),
    )
    _, _, leaving, gradient = lax.fori_loop(0, ticks, advance, initial)
    rim_terms = from_behind(gradient[:, :, tile_rows:].astype(jnp.bfloat16), "lat", 1).astype(
        jnp.float32
    )
    result = gradient[:, :, :tile_rows].at[:, :, :npix].add(rim_terms)
    return (leaving[None], result)


def solution(mesh):
    return jax.shard_map(
        body,
        mesh=mesh,
        in_specs=(
            P(),
            P(None, "lat", None),
            P("depth", "lat", None),
            P(),
            P("depth", "lat", None, None, None),
            P("lat", None, None),
        ),
        out_specs=(P("depth", "lat", None, None, None), P("depth", None, "lat", None)),
        check_vma=False,
    )
```

profile of v0, /device:TPU:0, one launch (start us, length us, event | category | flops | bytes accessed | tf_op | source)
XLA Modules:
  0.0 284.0 jit_solution(2128135463048121458)
XLA Ops:
  0.6 4.5 %collective-permute-start.2 = (bf16[1,256,512]{2,1,0:T(8,128)(2,1)}, bf16[1,256,512]{2,1,0:T(8,128)(2,1)S(1)}, u32[]{:S(2)}, u32[]{:S(2)}) collective-permute-start(bf16[1,256,512]{2,1,0:T(8,128)(2,1)} %param.20), channel_id=1, source_target_pairs={{0,7},{1,0},{2,1},{3,2},{4,3},{5,4},{6,5},{7,6},{8,15},{9,8},{10,9... | collective-permute-start | bytes 786440 | tf_op jit(solution)/shard_map/ppermute | solution.py:11
  9.5 3.7 %convert_cosine_fusion = (f32[1,1,512,512]{3,2,1,0:T(8,128)S(1)}, f32[1,1,512,512]{3,2,1,0:T(8,128)S(1)}) fusion(bf16[1,1,256,512]{3,2,1,0:T(8,128)(2,1)S(1)} %bitcast.369, bf16[1,1,256,512]{3,2,1,0:T(8,128)(2,1)S(1)} %bitcast.368), kind=kLoop, calls=%fused_computation.114 | loop fusion | flops 1048576 | bytes 2621440 | tf_op jit(solution)/shard_map/cos | solution.py:89
  13.2 1.5 pad_maximum_fusion.1
  16.5 1.6 broadcast_in_dim.32
  18.1 251.8 %while.28 = (s32[]{:T(128)}, bf16[2,256,256]{2,1,0:T(8,128)(2,1)}, bf16[2,256,256]{2,1,0:T(8,128)(2,1)S(1)}, bf16[4,2,256,256]{3,2,1,0:T(8,128)(2,1)}, f32[1,2,5...) while((s32[]{:T(128)}, bf16[2,256,256]{2,1,0:T(8,128)(2,1)}, ...), condition=%wide.region_7.8_spmd, body=%wide.region_0.7_spmd.sunk | while | flops 2156527616 | bytes 30148020 | solution.py:153
  18.1 8.3 %conditional.5 = (bf16[2,256,256]{2,1,0:T(8,128)(2,1)S(1)}) conditional(s32[]{:T(128)} %convert_element_type.241, () %tuple.94, (pred[]{:T(512)}, bf16[2,256,256]{2,1,0:T(8,128)(2,1)}, bf16[2,256,256]{2,1,0:T(8,128)(2,1)}, s32[2,4,2]{1,2,0:T(2,128)S(1)}, s32[]{:T(128)}, /*index=5*/f32[1,2,512,512]{3,2,1,0:T(8,128)}, ...), branch_computations={%region_1.1_spmd, %region_2.2_spmd} | conditional | flops 539623424 | bytes 6029433 | solution.py:111
  23.6 1.3 subtract_convert_fusion.1
  26.4 2.0 collective-permute-start
  32.3 5.8 %collective-permute-done.1 = bf16[2,256,256]{2,1,0:T(8,128)(2,1)S(1)} collective-permute-done((bf16[2,256,256]{2,1,0:T(8,128)(2,1)}, bf16[2,256,256]{2,1,0:T(8,128)(2,1)S(1)}, u32[]{:S(2)}, u32[]{:S(2)}) %collective-permute-start.1) | collective-permute-done | bytes 262176 | tf_op jit(solution)/shard_map/while/body/eval_jaxpr/ppermute | solution.py:17
  38.0 8.3 %conditional.5 = (bf16[2,256,256]{2,1,0:T(8,128)(2,1)S(1)}) conditional(s32[]{:T(128)} %convert_element_type.241, () %tuple.94, (pred[]{:T(512)}, bf16[2,256,256]{2,1,0:T(8,128)(2,1)}, bf16[2,256,256]{2,1,0:T(8,128)(2,1)}, s32[2,4,2]{1,2,0:T(2,128)S(1)}, s32[]{:T(128)}, /*index=5*/f32[1,2,512,512]{3,2,1,0:T(8,128)}, ...), branch_computations={%region_1.1_spmd, %region_2.2_spmd} | conditional | flops 539623424 | bytes 6029433 | solution.py:111
  43.5 1.3 subtract_convert_fusion.1
  46.3 2.3 collective-permute-start
  52.4 11.8 %collective-permute-done.1 = bf16[2,256,256]{2,1,0:T(8,128)(2,1)S(1)} collective-permute-done((bf16[2,256,256]{2,1,0:T(8,128)(2,1)}, bf16[2,256,256]{2,1,0:T(8,128)(2,1)S(1)}, u32[]{:S(2)}, u32[]{:S(2)}) %collective-permute-start.1) | collective-permute-done | bytes 262176 | tf_op jit(solution)/shard_map/while/body/eval_jaxpr/ppermute | solution.py:17
  64.1 8.3 %conditional.5 = (bf16[2,256,256]{2,1,0:T(8,128)(2,1)S(1)}) conditional(s32[]{:T(128)} %convert_element_type.241, () %tuple.94, (pred[]{:T(512)}, bf16[2,256,256]{2,1,0:T(8,128)(2,1)}, bf16[2,256,256]{2,1,0:T(8,128)(2,1)}, s32[2,4,2]{1,2,0:T(2,128)S(1)}, s32[]{:T(128)}, /*index=5*/f32[1,2,512,512]{3,2,1,0:T(8,128)}, ...), branch_computations={%region_1.1_spmd, %region_2.2_spmd} | conditional | flops 539623424 | bytes 6029433 | solution.py:111
  69.6 1.3 subtract_convert_fusion.1
  72.4 18.9 %collective-permute-start = (bf16[2,256,256]{2,1,0:T(8,128)(2,1)S(1)}, bf16[2,256,256]{2,1,0:T(8,128)(2,1)}, u32[]{:S(2)}, u32[]{:S(2)}) collective-permute-start(bf16[2,256,256]{2,1,0:T(8,128)(2,1)S(1)} %get-tuple-element.764), channel_id=1, source_target_pairs={{0,8},{8,16},{16,24},{1,9},{9,17},{17,25},{2,10},{10,18},{18,26},{... | collective-permute-start | bytes 786440 | tf_op jit(solution)/shard_map/while/body/eval_jaxpr/ppermute | solution.py:17
  95.1 23.1 %collective-permute-done.1 = bf16[2,256,256]{2,1,0:T(8,128)(2,1)S(1)} collective-permute-done((bf16[2,256,256]{2,1,0:T(8,128)(2,1)}, bf16[2,256,256]{2,1,0:T(8,128)(2,1)S(1)}, u32[]{:S(2)}, u32[]{:S(2)}) %collective-permute-start.1) | collective-permute-done | bytes 262176 | tf_op jit(solution)/shard_map/while/body/eval_jaxpr/ppermute | solution.py:17
  118.1 8.3 %conditional.5 = (bf16[2,256,256]{2,1,0:T(8,128)(2,1)S(1)}) conditional(s32[]{:T(128)} %convert_element_type.241, () %tuple.94, (pred[]{:T(512)}, bf16[2,256,256]{2,1,0:T(8,128)(2,1)}, bf16[2,256,256]{2,1,0:T(8,128)(2,1)}, s32[2,4,2]{1,2,0:T(2,128)S(1)}, s32[]{:T(128)}, /*index=5*/f32[1,2,512,512]{3,2,1,0:T(8,128)}, ...), branch_computations={%region_1.1_spmd, %region_2.2_spmd} | conditional | flops 539623424 | bytes 6029433 | solution.py:111
  123.6 1.3 subtract_convert_fusion.1
  126.4 5.5 %collective-permute-start = (bf16[2,256,256]{2,1,0:T(8,128)(2,1)S(1)}, bf16[2,256,256]{2,1,0:T(8,128)(2,1)}, u32[]{:S(2)}, u32[]{:S(2)}) collective-permute-start(bf16[2,256,256]{2,1,0:T(8,128)(2,1)S(1)} %get-tuple-element.764), channel_id=1, source_target_pairs={{0,8},{8,16},{16,24},{1,9},{9,17},{17,25},{2,10},{10,18},{18,26},{... | collective-permute-start | bytes 786440 | tf_op jit(solution)/shard_map/while/body/eval_jaxpr/ppermute | solution.py:17
  132.0 19.3 %conditional.6 = (bf16[2,256,256]{2,1,0:T(8,128)(2,1)}, f32[1,2,512,512]{3,2,1,0:T(8,128)}) conditional(s32[]{:T(128)} %convert_element_type.242, f32[1,2,512,512]{3,2,1,0:T(8,128)} %get-tuple-element.725, (s32[]{:T(128)}, s32[2,4,2]{1,2,0:T(2,128)S(1)}, f32[1,2,512,512]{3,2,1,0:T(8,128)}, s32[]{:T(128)}, bf16[1,4,2,256,256]{4,3,2,1,0:T(8,128)(2,1)}, ...), branch_computations={%region_3.3_spmd, %region_4.6_spmd} | conditional | flops 1616773120 | bytes 20709656 | solution.py:141
  136.9 1.3 subtract_convert_fusion.5
  141.6 1.4 multiply_add_fusion
  143.0 1.4 fusion.44
  145.1 6.2 %dynamic_update_slice.11 = f32[1,2,512,512]{3,2,1,0:T(8,128)} dynamic-update-slice(f32[1,2,512,512]{3,2,1,0:T(8,128)} %get-tuple-element.496, f32[1,2,256,256]{3,2,1,0:T(8,128)S(1)} %fusion.44, s32[]{:T(128)} %constant.121.clone, s32[]{:T(128)} %constant.121.clone, s32[]{:T(128)S(6)} %select_n.99, s32[]{:T(128)S(6)} %select_n.100) | dynamic-update-slice | bytes 1048580 | tf_op jit(solution)/shard_map/while/body/eval_jaxpr/cond/branch_1_fun/dynamic_update_slice | solution.py:139
  154.3 5.4 %collective-permute-done.1 = bf16[2,256,256]{2,1,0:T(8,128)(2,1)S(1)} collective-permute-done((bf16[2,256,256]{2,1,0:T(8,128)(2,1)}, bf16[2,256,256]{2,1,0:T(8,128)(2,1)S(1)}, u32[]{:S(2)}, u32[]{:S(2)}) %collective-permute-start.1) | collective-permute-done | bytes 262176 | tf_op jit(solution)/shard_map/while/body/eval_jaxpr/ppermute | solution.py:17
  159.8 11.5 %collective-permute-start = (bf16[2,256,256]{2,1,0:T(8,128)(2,1)S(1)}, bf16[2,256,256]{2,1,0:T(8,128)(2,1)}, u32[]{:S(2)}, u32[]{:S(2)}) collective-permute-start(bf16[2,256,256]{2,1,0:T(8,128)(2,1)S(1)} %get-tuple-element.764), channel_id=1, source_target_pairs={{0,8},{8,16},{16,24},{1,9},{9,17},{17,25},{2,10},{10,18},{18,26},{... | collective-permute-start | bytes 786440 | tf_op jit(solution)/shard_map/while/body/eval_jaxpr/ppermute | solution.py:17
  171.3 19.7 %conditional.6 = (bf16[2,256,256]{2,1,0:T(8,128)(2,1)}, f32[1,2,512,512]{3,2,1,0:T(8,128)}) conditional(s32[]{:T(128)} %convert_element_type.242, f32[1,2,512,512]{3,2,1,0:T(8,128)} %get-tuple-element.725, (s32[]{:T(128)}, s32[2,4,2]{1,2,0:T(2,128)S(1)}, f32[1,2,512,512]{3,2,1,0:T(8,128)}, s32[]{:T(128)}, bf16[1,4,2,256,256]{4,3,2,1,0:T(8,128)(2,1)}, ...), branch_computations={%region_3.3_spmd, %region_4.6_spmd} | conditional | flops 1616773120 | bytes 20709656 | solution.py:141
  176.3 1.3 subtract_convert_fusion.5
  180.9 1.4 multiply_add_fusion
  182.3 1.4 fusion.44
  184.4 6.6 %dynamic_update_slice.11 = f32[1,2,512,512]{3,2,1,0:T(8,128)} dynamic-update-slice(f32[1,2,512,512]{3,2,1,0:T(8,128)} %get-tuple-element.496, f32[1,2,256,256]{3,2,1,0:T(8,128)S(1)} %fusion.44, s32[]{:T(128)} %constant.121.clone, s32[]{:T(128)} %constant.121.clone, s32[]{:T(128)S(6)} %select_n.99, s32[]{:T(128)S(6)} %select_n.100) | dynamic-update-slice | bytes 1048580 | tf_op jit(solution)/shard_map/while/body/eval_jaxpr/cond/branch_1_fun/dynamic_update_slice | solution.py:139
  194.0 5.4 %collective-permute-done.1 = bf16[2,256,256]{2,1,0:T(8,128)(2,1)S(1)} collective-permute-done((bf16[2,256,256]{2,1,0:T(8,128)(2,1)}, bf16[2,256,256]{2,1,0:T(8,128)(2,1)S(1)}, u32[]{:S(2)}, u32[]{:S(2)}) %collective-permute-start.1) | collective-permute-done | bytes 262176 | tf_op jit(solution)/shard_map/while/body/eval_jaxpr/ppermute | solution.py:17
  199.5 2.9 %collective-permute-start = (bf16[2,256,256]{2,1,0:T(8,128)(2,1)S(1)}, bf16[2,256,256]{2,1,0:T(8,128)(2,1)}, u32[]{:S(2)}, u32[]{:S(2)}) collective-permute-start(bf16[2,256,256]{2,1,0:T(8,128)(2,1)S(1)} %get-tuple-element.764), channel_id=1, source_target_pairs={{0,8},{8,16},{16,24},{1,9},{9,17},{17,25},{2,10},{10,18},{18,26},{... | collective-permute-start | bytes 786440 | tf_op jit(solution)/shard_map/while/body/eval_jaxpr/ppermute | solution.py:17
  202.4 19.7 %conditional.6 = (bf16[2,256,256]{2,1,0:T(8,128)(2,1)}, f32[1,2,512,512]{3,2,1,0:T(8,128)}) conditional(s32[]{:T(128)} %convert_element_type.242, f32[1,2,512,512]{3,2,1,0:T(8,128)} %get-tuple-element.725, (s32[]{:T(128)}, s32[2,4,2]{1,2,0:T(2,128)S(1)}, f32[1,2,512,512]{3,2,1,0:T(8,128)}, s32[]{:T(128)}, bf16[1,4,2,256,256]{4,3,2,1,0:T(8,128)(2,1)}, ...), branch_computations={%region_3.3_spmd, %region_4.6_spmd} | conditional | flops 1616773120 | bytes 20709656 | solution.py:141
  207.4 1.3 subtract_convert_fusion.5
  212.0 1.4 multiply_add_fusion
  213.4 1.4 fusion.44
  215.5 6.6 %dynamic_update_slice.11 = f32[1,2,512,512]{3,2,1,0:T(8,128)} dynamic-update-slice(f32[1,2,512,512]{3,2,1,0:T(8,128)} %get-tuple-element.496, f32[1,2,256,256]{3,2,1,0:T(8,128)S(1)} %fusion.44, s32[]{:T(128)} %constant.121.clone, s32[]{:T(128)} %constant.121.clone, s32[]{:T(128)S(6)} %select_n.99, s32[]{:T(128)S(6)} %select_n.100) | dynamic-update-slice | bytes 1048580 | tf_op jit(solution)/shard_map/while/body/eval_jaxpr/cond/branch_1_fun/dynamic_update_slice | solution.py:139
  225.2 12.6 %collective-permute-done.1 = bf16[2,256,256]{2,1,0:T(8,128)(2,1)S(1)} collective-permute-done((bf16[2,256,256]{2,1,0:T(8,128)(2,1)}, bf16[2,256,256]{2,1,0:T(8,128)(2,1)S(1)}, u32[]{:S(2)}, u32[]{:S(2)}) %collective-permute-start.1) | collective-permute-done | bytes 262176 | tf_op jit(solution)/shard_map/while/body/eval_jaxpr/ppermute | solution.py:17
  237.8 4.1 %collective-permute-start = (bf16[2,256,256]{2,1,0:T(8,128)(2,1)S(1)}, bf16[2,256,256]{2,1,0:T(8,128)(2,1)}, u32[]{:S(2)}, u32[]{:S(2)}) collective-permute-start(bf16[2,256,256]{2,1,0:T(8,128)(2,1)S(1)} %get-tuple-element.764), channel_id=1, source_target_pairs={{0,8},{8,16},{16,24},{1,9},{9,17},{17,25},{2,10},{10,18},{18,26},{... | collective-permute-start | bytes 786440 | tf_op jit(solution)/shard_map/while/body/eval_jaxpr/ppermute | solution.py:17
  241.9 19.6 %conditional.6 = (bf16[2,256,256]{2,1,0:T(8,128)(2,1)}, f32[1,2,512,512]{3,2,1,0:T(8,128)}) conditional(s32[]{:T(128)} %convert_element_type.242, f32[1,2,512,512]{3,2,1,0:T(8,128)} %get-tuple-element.725, (s32[]{:T(128)}, s32[2,4,2]{1,2,0:T(2,128)S(1)}, f32[1,2,512,512]{3,2,1,0:T(8,128)}, s32[]{:T(128)}, bf16[1,4,2,256,256]{4,3,2,1,0:T(8,128)(2,1)}, ...), branch_computations={%region_3.3_spmd, %region_4.6_spmd} | conditional | flops 1616773120 | bytes 20709656 | solution.py:141
  251.5 1.4 multiply_add_fusion
  252.8 1.4 fusion.44
  254.9 6.5 %dynamic_update_slice.11 = f32[1,2,512,512]{3,2,1,0:T(8,128)} dynamic-update-slice(f32[1,2,512,512]{3,2,1,0:T(8,128)} %get-tuple-element.496, f32[1,2,256,256]{3,2,1,0:T(8,128)S(1)} %fusion.44, s32[]{:T(128)} %constant.121.clone, s32[]{:T(128)} %constant.121.clone, s32[]{:T(128)S(6)} %select_n.99, s32[]{:T(128)S(6)} %select_n.100) | dynamic-update-slice | bytes 1048580 | tf_op jit(solution)/shard_map/while/body/eval_jaxpr/cond/branch_1_fun/dynamic_update_slice | solution.py:139
  264.5 5.4 %collective-permute-done.1 = bf16[2,256,256]{2,1,0:T(8,128)(2,1)S(1)} collective-permute-done((bf16[2,256,256]{2,1,0:T(8,128)(2,1)}, bf16[2,256,256]{2,1,0:T(8,128)(2,1)S(1)}, u32[]{:S(2)}, u32[]{:S(2)}) %collective-permute-start.1) | collective-permute-done | bytes 262176 | tf_op jit(solution)/shard_map/while/body/eval_jaxpr/ppermute | solution.py:17
  271.3 10.4 %collective-permute-done.3 = bf16[1,2,256,512]{3,2,1,0:T(8,128)(2,1)S(1)} collective-permute-done((bf16[1,2,256,512]{3,2,1,0:T(8,128)(2,1)S(1)}, bf16[1,2,256,512]{3,2,1,0:T(8,128)(2,1)S(1)}, u32[]{:S(2)}, u32[]{:S(2)}) %collective-permute-start.3) | collective-permute-done | bytes 524320 | tf_op jit(solution)/shard_map/ppermute | solution.py:11
  281.7 2.4 convert_add_fusion
  (127 shorter events, 69.1 us)
Async XLA Ops:
  0.6 7.7 %copy-start = (f32[256,256]{1,0:T(8,128)S(1)}, f32[256,256]{1,0:T(8,128)}, u32[]{:S(2)}) copy-start(f32[256,256]{1,0:T(8,128)} %param.21) | copy-start | bytes 786436
  0.6 8.9 %collective-permute-start.2 = (bf16[1,256,512]{2,1,0:T(8,128)(2,1)}, bf16[1,256,512]{2,1,0:T(8,128)(2,1)S(1)}, u32[]{:S(2)}, u32[]{:S(2)}) collective-permute-start(bf16[1,256,512]{2,1,0:T(8,128)(2,1)} %param.20), channel_id=1, source_target_pairs={{0,7},{1,0},{2,1},{3,2},{4,3},{5,4},{6,5},{7,6},{8,15},{9,8},{10,9... | collective-permute-start | bytes 786440 | tf_op jit(solution)/shard_map/ppermute | solution.py:11
  8.2 1.4 copy-start.1
  14.7 3.4 %copy-start.2 = (s32[2,4,2]{1,2,0:T(2,128)S(1)}, s32[2,4,2]{1,2,0:T(2,128)}, u32[]{:S(2)}) copy-start(s32[2,4,2]{1,2,0:T(2,128)} %param.19) | copy-start | bytes 196
  26.4 5.8 %collective-permute-start = (bf16[2,256,256]{2,1,0:T(8,128)(2,1)S(1)}, bf16[2,256,256]{2,1,0:T(8,128)(2,1)}, u32[]{:S(2)}, u32[]{:S(2)}) collective-permute-start(bf16[2,256,256]{2,1,0:T(8,128)(2,1)S(1)} %get-tuple-element.764), channel_id=1, source_target_pairs={{0,8},{8,16},{16,24},{1,9},{9,17},{17,25},{2,10},{10,18},{18,26},{... | collective-permute-start | bytes 786440 | tf_op jit(solution)/shard_map/while/body/eval_jaxpr/ppermute | solution.py:17
  29.2 8.8 %collective-permute-start.1 = (bf16[2,256,256]{2,1,0:T(8,128)(2,1)}, bf16[2,256,256]{2,1,0:T(8,128)(2,1)S(1)}, u32[]{:S(2)}, u32[]{:S(2)}) collective-permute-start(bf16[2,256,256]{2,1,0:T(8,128)(2,1)} %get-tuple-element.694), channel_id=1, source_target_pairs={{8,0},{16,8},{24,16},{9,1},{17,9},{25,17},{10,2},{18,10},{26,18},{... | collective-permute-start | bytes 786440 | tf_op jit(solution)/shard_map/while/body/eval_jaxpr/ppermute | solution.py:17
  46.3 6.0 %collective-permute-start = (bf16[2,256,256]{2,1,0:T(8,128)(2,1)S(1)}, bf16[2,256,256]{2,1,0:T(8,128)(2,1)}, u32[]{:S(2)}, u32[]{:S(2)}) collective-permute-start(bf16[2,256,256]{2,1,0:T(8,128)(2,1)S(1)} %get-tuple-element.764), channel_id=1, source_target_pairs={{0,8},{8,16},{16,24},{1,9},{9,17},{17,25},{2,10},{10,18},{18,26},{... | collective-permute-start | bytes 786440 | tf_op jit(solution)/shard_map/while/body/eval_jaxpr/ppermute | solution.py:17
  49.3 14.8 %collective-permute-start.1 = (bf16[2,256,256]{2,1,0:T(8,128)(2,1)}, bf16[2,256,256]{2,1,0:T(8,128)(2,1)S(1)}, u32[]{:S(2)}, u32[]{:S(2)}) collective-permute-start(bf16[2,256,256]{2,1,0:T(8,128)(2,1)} %get-tuple-element.694), channel_id=1, source_target_pairs={{8,0},{16,8},{24,16},{9,1},{17,9},{25,17},{10,2},{18,10},{26,18},{... | collective-permute-start | bytes 786440 | tf_op jit(solution)/shard_map/while/body/eval_jaxpr/ppermute | solution.py:17
  72.4 22.6 %collective-permute-start = (bf16[2,256,256]{2,1,0:T(8,128)(2,1)S(1)}, bf16[2,256,256]{2,1,0:T(8,128)(2,1)}, u32[]{:S(2)}, u32[]{:S(2)}) collective-permute-start(bf16[2,256,256]{2,1,0:T(8,128)(2,1)S(1)} %get-tuple-element.764), channel_id=1, source_target_pairs={{0,8},{8,16},{16,24},{1,9},{9,17},{17,25},{2,10},{10,18},{18,26},{... | collective-permute-start | bytes 786440 | tf_op jit(solution)/shard_map/while/body/eval_jaxpr/ppermute | solution.py:17
  92.0 26.1 %collective-permute-start.1 = (bf16[2,256,256]{2,1,0:T(8,128)(2,1)}, bf16[2,256,256]{2,1,0:T(8,128)(2,1)S(1)}, u32[]{:S(2)}, u32[]{:S(2)}) collective-permute-start(bf16[2,256,256]{2,1,0:T(8,128)(2,1)} %get-tuple-element.694), channel_id=1, source_target_pairs={{8,0},{16,8},{24,16},{9,1},{17,9},{25,17},{10,2},{18,10},{26,18},{... | collective-permute-start | bytes 786440 | tf_op jit(solution)/shard_map/while/body/eval_jaxpr/ppermute | solution.py:17
  126.4 27.9 %collective-permute-start = (bf16[2,256,256]{2,1,0:T(8,128)(2,1)S(1)}, bf16[2,256,256]{2,1,0:T(8,128)(2,1)}, u32[]{:S(2)}, u32[]{:S(2)}) collective-permute-start(bf16[2,256,256]{2,1,0:T(8,128)(2,1)S(1)} %get-tuple-element.764), channel_id=1, source_target_pairs={{0,8},{8,16},{16,24},{1,9},{9,17},{17,25},{2,10},{10,18},{18,26},{... | collective-permute-start | bytes 786440 | tf_op jit(solution)/shard_map/while/body/eval_jaxpr/ppermute | solution.py:17
  151.3 8.5 %collective-permute-start.1 = (bf16[2,256,256]{2,1,0:T(8,128)(2,1)}, bf16[2,256,256]{2,1,0:T(8,128)(2,1)S(1)}, u32[]{:S(2)}, u32[]{:S(2)}) collective-permute-start(bf16[2,256,256]{2,1,0:T(8,128)(2,1)} %get-tuple-element.694), channel_id=1, source_target_pairs={{8,0},{16,8},{24,16},{9,1},{17,9},{25,17},{10,2},{18,10},{26,18},{... | collective-permute-start | bytes 786440 | tf_op jit(solution)/shard_map/while/body/eval_jaxpr/ppermute | solution.py:17
  159.8 34.2 %collective-permute-start = (bf16[2,256,256]{2,1,0:T(8,128)(2,1)S(1)}, bf16[2,256,256]{2,1,0:T(8,128)(2,1)}, u32[]{:S(2)}, u32[]{:S(2)}) collective-permute-start(bf16[2,256,256]{2,1,0:T(8,128)(2,1)S(1)} %get-tuple-element.764), channel_id=1, source_target_pairs={{0,8},{8,16},{16,24},{1,9},{9,17},{17,25},{2,10},{10,18},{18,26},{... | collective-permute-start | bytes 786440 | tf_op jit(solution)/shard_map/while/body/eval_jaxpr/ppermute | solution.py:17
  191.0 8.5 %collective-permute-start.1 = (bf16[2,256,256]{2,1,0:T(8,128)(2,1)}, bf16[2,256,256]{2,1,0:T(8,128)(2,1)S(1)}, u32[]{:S(2)}, u32[]{:S(2)}) collective-permute-start(bf16[2,256,256]{2,1,0:T(8,128)(2,1)} %get-tuple-element.694), channel_id=1, source_target_pairs={{8,0},{16,8},{24,16},{9,1},{17,9},{25,17},{10,2},{18,10},{26,18},{... | collective-permute-start | bytes 786440 | tf_op jit(solution)/shard_map/while/body/eval_jaxpr/ppermute | solution.py:17
  199.5 25.7 %collective-permute-start = (bf16[2,256,256]{2,1,0:T(8,128)(2,1)S(1)}, bf16[2,256,256]{2,1,0:T(8,128)(2,1)}, u32[]{:S(2)}, u32[]{:S(2)}) collective-permute-start(bf16[2,256,256]{2,1,0:T(8,128)(2,1)S(1)} %get-tuple-element.764), channel_id=1, source_target_pairs={{0,8},{8,16},{16,24},{1,9},{9,17},{17,25},{2,10},{10,18},{18,26},{... | collective-permute-start | bytes 786440 | tf_op jit(solution)/shard_map/while/body/eval_jaxpr/ppermute | solution.py:17
  222.1 15.7 %collective-permute-start.1 = (bf16[2,256,256]{2,1,0:T(8,128)(2,1)}, bf16[2,256,256]{2,1,0:T(8,128)(2,1)S(1)}, u32[]{:S(2)}, u32[]{:S(2)}) collective-permute-start(bf16[2,256,256]{2,1,0:T(8,128)(2,1)} %get-tuple-element.694), channel_id=1, source_target_pairs={{8,0},{16,8},{24,16},{9,1},{17,9},{25,17},{10,2},{18,10},{26,18},{... | collective-permute-start | bytes 786440 | tf_op jit(solution)/shard_map/while/body/eval_jaxpr/ppermute | solution.py:17
  237.8 26.7 %collective-permute-start = (bf16[2,256,256]{2,1,0:T(8,128)(2,1)S(1)}, bf16[2,256,256]{2,1,0:T(8,128)(2,1)}, u32[]{:S(2)}, u32[]{:S(2)}) collective-permute-start(bf16[2,256,256]{2,1,0:T(8,128)(2,1)S(1)} %get-tuple-element.764), channel_id=1, source_target_pairs={{0,8},{8,16},{16,24},{1,9},{9,17},{17,25},{2,10},{10,18},{18,26},{... | collective-permute-start | bytes 786440 | tf_op jit(solution)/shard_map/while/body/eval_jaxpr/ppermute | solution.py:17
  261.4 8.5 %collective-permute-start.1 = (bf16[2,256,256]{2,1,0:T(8,128)(2,1)}, bf16[2,256,256]{2,1,0:T(8,128)(2,1)S(1)}, u32[]{:S(2)}, u32[]{:S(2)}) collective-permute-start(bf16[2,256,256]{2,1,0:T(8,128)(2,1)} %get-tuple-element.694), channel_id=1, source_target_pairs={{8,0},{16,8},{24,16},{9,1},{17,9},{25,17},{10,2},{18,10},{26,18},{... | collective-permute-start | bytes 786440 | tf_op jit(solution)/shard_map/while/body/eval_jaxpr/ppermute | solution.py:17
  271.2 10.5 %collective-permute-start.3 = (bf16[1,2,256,512]{3,2,1,0:T(8,128)(2,1)S(1)}, bf16[1,2,256,512]{3,2,1,0:T(8,128)(2,1)S(1)}, u32[]{:S(2)}, u32[]{:S(2)}) collective-permute-start(bf16[1,2,256,512]{3,2,1,0:T(8,128)(2,1)S(1)} %slice.254), channel_id=1, source_target_pairs={{0,1},{1,2},{2,3},{3,4},{4,5},{5,6},{6,7},{7,0},{8,9},{9,10},{10,1... | collective-permute-start | bytes 1572872 | tf_op jit(solution)/shard_map/ppermute | solution.py:11
where the time goes:
time: 288 us; the launch traced here: 284 us
  waiting for transfers between devices  79.9 us (28%)
  starting transfers between devices  60.8 us (21%)
  other arithmetic  49.7 us (17%)
  local copies, waits for them, and re-layouts  46.8 us (16%)
  loops' own time  29.4 us (10%)
  matrix products  16.7 us (6%)
    ppermute x14, waiting for transfers between devices, shifted_2(): return lax.ppermute(block, axis, route)  69.5 us
    ppermute x14, starting transfers between devices, shifted_2(): return lax.ppermute(block, axis, route)  56.2 us
    dynamic_update_slice x4, local copies, waits for them, and re-layouts, run_behind(): return (adjoint, lax.dynamic_update_slice(gradient, summed, corner))  26 us
    another operation x7, loops' own time, advance(): ahead_out = lax.cond(ahead_live, run_ahead, lambda: empty_wave)  15.3 us
    dot_general x24, matrix products, transform(): jnp.einsum('bjk,abkl->ajl', left, table, preferred_element_type=jnp.float32)  15.3 us
    another operation x7, loops' own time, advance(): lax.cond(behind_live, run_behind, lambda: (empty_wave, gradient))  13.9 us
    another operation x11, other arithmetic  13.8 us
    ppermute x2, waiting for transfers between devices, from_behind(): lax.ppermute(x, axis, [(i, (i + by) % devices) for i in range(devices)])  10.4 us
  transfers between devices with their start and end apart: 16, of which 8 were waited for; matrix products, arithmetic and copies ran while one was open for 29% of the time, Pallas kernels for 0%

commit v1 on v0

v1 whole, which is shorter than its diff:
```python
import functools
import math

import jax
import jax.numpy as jnp
import numpy as np
from jax import lax
from jax.experimental import pallas as pl
from jax.experimental.pallas import tpu as pltpu
from jax.sharding import PartitionSpec as P

MESH = pl.DeviceIdType.MESH
F32 = jnp.float32
BF16 = jnp.bfloat16


def tables(n):
    counter = np.arange(n)
    angles = 2.0 * math.pi / n * (counter[:, None] * counter[None, :] % n)
    re = np.cos(angles) / math.sqrt(n)
    im = -np.sin(angles) / math.sqrt(n)
    ahead = np.block([[re, -im], [im, re]])
    back = np.block([[re, im], [-im, re]])
    return ahead.astype(BF16), back.astype(BF16)


def fit(function, terms):
    top = (math.pi + 1e-3) ** 2
    u = (np.cos(np.pi * (np.arange(400) + 0.5) / 400) + 1) * top / 2
    poly = np.polynomial.Chebyshev.fit(u, function(np.sqrt(u)), terms - 1, domain=[0, top])
    return [float(v) for v in poly.convert(kind=np.polynomial.Polynomial).coef]


SIN = fit(lambda x: np.sin(x) / x, 7)
COS = fit(np.cos, 8)


def horner(coefs, u):
    value = jnp.full_like(u, coefs[-1])
    for coef in coefs[-2::-1]:
        value = value * u + coef
    return value


def cos_sin(x):
    u = x * x
    return horner(COS, u), x * horner(SIN, u)


def rows_to_lanes(x):
    half = x.shape[0] // 2
    return jnp.concatenate([x[:half], x[half:]], axis=1)


def pair(re, im):
    return jnp.concatenate([re.astype(BF16), im.astype(BF16)], axis=0)


def kernel(D, N, Pn, pos, a_ref, b_ref, probe, tile, prop, stored, measured,
           leaving, grad,
           tiles, nexts, h_ref, waves, rolled, st3, ge_out, ge_in, own, nxt, rim_out, rim_in,
           t_send, t_recv, n_send, n_recv, s_send, s_recv, g_send, g_recv, r_send, r_recv):
    n = prop.shape[0]
    slots = st3.shape[0]
    d = lax.axis_index("depth")
    l = lax.axis_index("lat")
    before = lax.rem(l + N - 1, N)
    after = lax.rem(l + 1, N)

    def remote(src, dst, send, recv, depth, lat):
        return pltpu.make_async_remote_copy(
            src_ref=src, dst_ref=dst, send_sem=send, recv_sem=recv,
            device_id=(depth, lat), device_id_type=MESH)

    barrier = pltpu.get_barrier_semaphore()
    for off in range(1, D):
        pl.semaphore_signal(barrier, inc=1, device_id=(lax.rem(d + off, D), l), device_id_type=MESH)
    for other in (before, after):
        pl.semaphore_signal(barrier, inc=1, device_id=(d, other), device_id_type=MESH)
    pl.semaphore_wait(barrier, D + 1)

    def send_tile(j):
        return remote(tile, tiles.at[d], t_send.at[j], t_recv.at[d], j, l)

    def recv_tile(k):
        return remote(tile, tiles.at[k], t_send.at[k], t_recv.at[k], d, l)

    def pass_on(k, source):
        return remote(source, nexts.at[k], n_send.at[k], n_recv.at[k], d, before)

    def send_stored(q):
        return remote(stored.at[q], st3.at[q // D], s_send.at[q], s_recv.at[q // D], q % D, l)

    pass_on(d, tile).start()
    for off in range(1, D):
        send_tile(lax.rem(d + off, D)).start()

    @pl.when(d == D - 1)
    def _():
        for q in range(Pn):
            if q % D != D - 1:
                send_stored(q).start()
            else:
                st3[q // D] = stored[q]

    tiles[d] = tile[...]
    c, s = cos_sin(prop[...])
    h_ref[0] = c
    h_ref[1] = s

    row = lax.broadcasted_iota(jnp.int32, (n, n), 0)
    col = lax.broadcasted_iota(jnp.int32, (n, n), 1)

    def shift(lead, by):
        at = lead + by
        at = jnp.where(at < 0, at + n, at)
        return jnp.where(at >= n, at - n, at)

    def one_hot(where):
        return jnp.where(where, 1.0, 0.0).astype(BF16)

    def move(wave, left, right):
        turned = jnp.dot(wave, right, preferred_element_type=F32).astype(BF16)
        return (jnp.dot(left, turned[:n], preferred_element_type=F32).astype(BF16),
                jnp.dot(left, turned[n:], preferred_element_type=F32).astype(BF16))

    def roll_in(wave, r, c):
        left = one_hot(col == shift(row, -r))
        right = one_hot(row == shift(col, -c))
        return move(wave, left, right)

    def roll_out(wave, r, c):
        left = one_hot(col == shift(row, r))
        right = one_hot(row == shift(col, c))
        return move(wave, left, right)

    @pl.loop(0, Pn)
    def _(q):
        re, im = roll_in(probe[...].reshape(2 * n, n), pos[0, q, 0], pos[0, q, 1])
        waves[q, :n] = re
        waves[q, n:] = im
        re, im = roll_in(stored[q].reshape(2 * n, n), pos[1, q, 0], pos[1, q, 1])
        rolled[q, :n] = re
        rolled[q, n:] = im

    for off in range(1, D):
        k = lax.rem(d + off, D)
        recv_tile(k).wait_recv()
        pass_on(k, tiles.at[k]).start()
    for off in range(D):
        k = lax.rem(d + off, D)
        pass_on(k, tiles.at[k]).wait_recv()

    def dft(wave):
        left = jnp.dot(a_ref[...], wave, preferred_element_type=F32).astype(BF16)
        out = jnp.dot(rows_to_lanes(left), b_ref[...], preferred_element_type=F32)
        return out[:, :n], out[:, n:]

    def idft(wave):
        left = jnp.dot(b_ref[...], wave, preferred_element_type=F32).astype(BF16)
        out = jnp.dot(rows_to_lanes(left), a_ref[...], preferred_element_type=F32)
        return out[:, :n], out[:, n:]

    def transmission(k, r, c):
        right = col < c
        here = jnp.where(right, tiles[k, :, n:].astype(F32), tiles[k, :, :n].astype(F32))
        there = jnp.where(right, nexts[k, :, n:].astype(F32), nexts[k, :, :n].astype(F32))
        return cos_sin(jnp.where(row < r, there, here))

    def through(re, im, t):
        tr, ti = t
        fr, fi = dft(pair(re * tr - im * ti, re * ti + im * tr))
        hr, hi = h_ref[0], h_ref[1]
        return idft(pair(hr * fr - hi * fi, hr * fi + hi * fr))

    def send_ge(slot, k, q):
        return remote(ge_out.at[slot, k], ge_in.at[q], g_send.at[slot, k], g_recv.at[q], k, l)

    def backward(slot):
        q = slot * D + d
        r = pos[1, q, 0]
        c = pos[1, q, 1]

        @pl.when(d != D - 1)
        def _():
            remote(stored.at[q], st3.at[slot], s_send.at[q], s_recv.at[slot], d, l).wait_recv()

        re, im = roll_in(st3[slot].reshape(2 * n, n), r, c)
        xr, xi = through(re.astype(F32), im.astype(F32), transmission(D - 1, r, c))
        fr, fi = dft(pair(xr, xi))
        weight = fr * fr + fi * fi - measured[q]
        gr, gi = idft(pair(weight * fr, weight * fi))

        def step(i, g):
            k = D - 1 - i
            fr, fi = dft(g)
            hr, hi = h_ref[0], h_ref[1]
            er, ei = idft(pair(hr * fr + hi * fi, hr * fi - hi * fr))
            ge_out[slot, k] = pair(er, ei)

            @pl.when(k == d)
            def _():
                ge_in[q] = pair(er, ei)

            @pl.when(k != d)
            def _():
                send_ge(slot, k, q).start()

            tr, ti = transmission(k, r, c)
            return pair(tr * er + ti * ei, tr * ei - ti * er)

        lax.fori_loop(0, D, step, pair(gr, gi))

    for slot in range(slots):
        if (slot + 1) * D <= Pn:
            backward(slot)
        else:
            pl.when(slot * D + d < Pn)(functools.partial(backward, slot))

    def forward(k, _):
        def one(p, _):
            wave = waves[p].astype(F32)
            re, im = through(wave[:n], wave[n:], transmission(k, pos[0, p, 0], pos[0, p, 1]))
            waves[p] = pair(re, im)
            return 0

        return lax.fori_loop(0, Pn, one, 0)

    lax.fori_loop(0, d + 1, forward, 0)

    @pl.loop(0, Pn)
    def _(p):
        re, im = roll_out(waves[p], pos[0, p, 0], pos[0, p, 1])
        leaving[p, 0] = re
        leaving[p, 1] = im

    for q in range(Pn):
        @pl.when(d != q % D)
        def _():
            remote(ge_out.at[0, 0], ge_in.at[q], g_send.at[0, 0], g_recv.at[q], d, l).wait_recv()

        u = rolled[q].astype(F32)
        g = ge_in[q].astype(F32)
        ur, ui, gr, gi = u[:n], u[n:], g[:n], g[n:]
        lower = row < pos[1, q, 0]
        right = col < pos[1, q, 1]
        for part, term in enumerate((ur * gr + ui * gi, ur * gi - ui * gr)):
            here = jnp.where(lower, 0.0, term)
            there = jnp.where(lower, term, 0.0)
            for target, value in ((own, here), (nxt, there)):
                west = jnp.where(right, 0.0, value)
                east = jnp.where(right, value, 0.0)
                if q > 0:
                    west = west + target[part, :, :n]
                    east = east + target[part, :, n:]
                target[part, :, :n] = west
                target[part, :, n:] = east

    rim_out[...] = nxt[...].astype(BF16)
    rim = remote(rim_out, rim_in, r_send, r_recv, d, after)
    rim.start()

    for off in range(1, D):
        send_tile(lax.rem(d + off, D)).wait_send()
    for k in range(D):
        pass_on(k, tiles.at[k]).wait_send()

    @pl.when(d == D - 1)
    def _():
        for q in range(Pn):
            if q % D != D - 1:
                send_stored(q).wait_send()

    for slot in range(slots):
        def drain(slot=slot):
            for off in range(1, D):
                send_ge(slot, lax.rem(d + off, D), slot * D + d).wait_send()
        pl.when(slot * D + d < Pn)(drain)

    rim.wait()
    grad[...] = own[...] + rim_in[...].astype(F32)


def body(probe, positions, object_phase, propagator, stored, measured):
    n = probe.shape[-1]
    sections, rows, columns = object_phase.shape
    assert sections == 1 and rows == n and columns == 2 * n
    Pn = positions.shape[1]
    D = lax.axis_size("depth")
    N = lax.axis_size("lat")
    slots = -(-Pn // D)
    ahead, back = tables(n)
    vmem = pl.BlockSpec(memory_space=pltpu.VMEM)
    smem = pl.BlockSpec(memory_space=pltpu.SMEM)
    dma = pltpu.SemaphoreType.DMA
    leaving, grad = pl.pallas_call(
        functools.partial(kernel, D, N, Pn),
        out_shape=(
            jax.ShapeDtypeStruct((Pn, 2, n, n), BF16),
            jax.ShapeDtypeStruct((2, n, 2 * n), F32),
        ),
        in_specs=[smem] + [vmem] * 7,
        out_specs=(vmem, vmem),
        scratch_shapes=[
            pltpu.VMEM((D, n, 2 * n), BF16),
            pltpu.VMEM((D, n, 2 * n), BF16),
            pltpu.VMEM((2, n, n), F32),
            pltpu.VMEM((Pn, 2 * n, n), BF16),
            pltpu.VMEM((Pn, 2 * n, n), BF16),
            pltpu.VMEM((slots, 2, n, n), BF16),
            pltpu.VMEM((slots, D, 2 * n, n), BF16),
            pltpu.VMEM((Pn, 2 * n, n), BF16),
            pltpu.VMEM((2, n, 2 * n), F32),
            pltpu.VMEM((2, n, 2 * n), F32),
            pltpu.VMEM((2, n, 2 * n), BF16),
            pltpu.VMEM((2, n, 2 * n), BF16),
            dma((D,)), dma((D,)),
            dma((D,)), dma((D,)),
            dma((Pn,)), dma((slots,)),
            dma((slots, D)), dma((Pn,)),
            dma, dma,
        ],
        compiler_params=pltpu.CompilerParams(
            collective_id=0, has_side_effects=True, vmem_limit_bytes=48 << 20),
        cost_estimate=pl.CostEstimate(
            flops=(2 * D * Pn + 4 * D) * 16 * n ** 3, bytes_accessed=32 * n * n * 2 * Pn, transcendentals=0),
    )(positions, ahead, back, probe, object_phase[0], propagator, stored[0], measured)
    return leaving[None], grad[None]


def solution(mesh):
    return jax.shard_map(
        body,
        mesh=mesh,
        in_specs=(
            P(),
            P(None, "lat", None),
            P("depth", "lat", None),
            P(),
            P("depth", "lat", None, None, None),
            P("lat", None, None),
        ),
        out_specs=(P("depth", "lat", None, None, None), P("depth", None, "lat", None)),
        check_vma=False,
    )
```

time: 288 us -> 87.6 us (0.30)
  the two profiles are of different devices: /device:TPU:0 before, /device:TPU:6 now
where the time goes in v1:
time: 87.6 us; the launch traced here: 87.2 us
  Pallas kernels  76.4 us (87%)
  local copies, waits for them, and re-layouts  10.1 us (12%)
    pallas_call x1, Pallas kernels, body(): pl.pallas_call(functools.partial(kernel, D, N, Pn), out_shape=(jax.ShapeD...  76.4 us
    unnamed x19, local copies, waits for them, and re-layouts  10.1 us

profile of v1, /device:TPU:6, one launch (start us, length us, event | category | flops | bytes accessed | tf_op | source)
XLA Modules:
  0.0 87.2 jit_solution(13276515619202815555)
XLA Ops:
  0.6 0.0 copy-start.7
  0.6 0.7 copy-done.7
  1.3 0.1 copy.10.pos
  1.4 0.0 copy-start
  1.4 1.2 %copy-done = bf16[1,4,2,256,256]{4,3,2,1,0:T(8,128)(2,1)S(1)} copy-done((bf16[1,4,2,256,256]{4,3,2,1,0:T(8,128)(2,1)S(1)}, bf16[1,4,2,256,256]{4,3,2,1,0:T(8,128)(2,1)}, u32[]{:S(2)}) %copy-start) | copy-done | bytes 1048600
  2.6 0.0 copy-start.1
  2.6 1.2 %copy-done.1 = f32[4,256,256]{2,1,0:T(8,128)S(1)} copy-done((f32[4,256,256]{2,1,0:T(8,128)S(1)}, f32[4,256,256]{2,1,0:T(8,128)}, u32[]{:S(2)}) %copy-start.1) | copy-done | bytes 1048600
  3.9 0.0 copy-start.2
  3.9 0.9 %copy-done.2 = bf16[2,256,256]{2,1,0:T(8,128)(2,1)S(1)} copy-done((bf16[2,256,256]{2,1,0:T(8,128)(2,1)S(1)}, bf16[2,256,256]{2,1,0:T(8,128)(2,1)}, u32[]{:S(2)}) %copy-start.2) | copy-done | bytes 262168
  4.8 0.0 copy-start.3
  4.8 0.9 %copy-done.3 = bf16[1,256,512]{2,1,0:T(8,128)(2,1)S(1)} copy-done((bf16[1,256,512]{2,1,0:T(8,128)(2,1)S(1)}, bf16[1,256,512]{2,1,0:T(8,128)(2,1)}, u32[]{:S(2)}) %copy-start.3) | copy-done | bytes 262168
  5.8 0.0 copy-start.4
  5.8 0.9 %copy-done.4 = f32[256,256]{1,0:T(8,128)S(1)} copy-done((f32[256,256]{1,0:T(8,128)S(1)}, f32[256,256]{1,0:T(8,128)}, u32[]{:S(2)}) %copy-start.4) | copy-done | bytes 262168
  6.7 0.0 copy-start.5
  6.7 1.0 %copy-done.5 = bf16[512,512]{1,0:T(8,128)(2,1)S(1)} copy-done((bf16[512,512]{1,0:T(8,128)(2,1)S(1)}, bf16[512,512]{1,0:T(8,128)(2,1)}, u32[]{:S(2)}) %copy-start.5) | copy-done | bytes 524312
  7.8 0.0 copy-start.6
  7.8 1.0 %copy-done.6 = bf16[512,512]{1,0:T(8,128)(2,1)S(1)} copy-done((bf16[512,512]{1,0:T(8,128)(2,1)S(1)}, bf16[512,512]{1,0:T(8,128)(2,1)}, u32[]{:S(2)}) %copy-start.6) | copy-done | bytes 524312
  8.8 76.4 %shard_map.95 = (bf16[4,2,256,256]{3,2,1,0:T(8,128)(2,1)S(1)}, f32[2,256,512]{2,1,0:T(8,128)S(1)}) custom-call(s32[2,4,2]{2,1,0:T(4,128)S(1)} %copy.10.pos, bf16[512,512]{1,0:T(8,128)(2,1)S(1)} %copy-done.6, bf16[512,512]{1,0:T(8,128)(2,1)S(1)} %copy-done.5, bf16[2,256,256]{2,1,0:T(8,128)(2,1)S(1)} %copy-done.2, bf16[256,512]{1,0:T(8,128)(2,1)S(1)} %bitcast.7, ...), custom_call_target="tpu_custom_call" | custom-call | flops 12884901888 | bytes 16777216 | tf_op jit(solution)/shard_map/pallas_call | solution.py:296
  85.2 1.0 %copy.13 = bf16[1,4,2,256,256]{4,3,2,1,0:T(8,128)(2,1)} copy(bf16[1,4,2,256,256]{4,3,2,1,0:T(8,128)(2,1)S(1)} %bitcast.5) | data formatting | bytes 2097152
  86.2 1.0 %copy.14 = f32[1,2,256,512]{3,2,1,0:T(8,128)} copy(f32[1,2,256,512]{3,2,1,0:T(8,128)S(1)} %bitcast.4) | data formatting | bytes 2097152
Async XLA Ops:
  0.6 0.7 copy-start.7
  1.4 1.2 %copy-start = (bf16[1,4,2,256,256]{4,3,2,1,0:T(8,128)(2,1)S(1)}, bf16[1,4,2,256,256]{4,3,2,1,0:T(8,128)(2,1)}, u32[]{:S(2)}) copy-start(bf16[1,4,2,256,256]{4,3,2,1,0:T(8,128)(2,1)} %param.12) | copy-start | bytes 3145732
  2.6 1.2 %copy-start.1 = (f32[4,256,256]{2,1,0:T(8,128)S(1)}, f32[4,256,256]{2,1,0:T(8,128)}, u32[]{:S(2)}) copy-start(f32[4,256,256]{2,1,0:T(8,128)} %measured.1) | copy-start | bytes 3145732
  3.9 0.9 %copy-start.2 = (bf16[2,256,256]{2,1,0:T(8,128)(2,1)S(1)}, bf16[2,256,256]{2,1,0:T(8,128)(2,1)}, u32[]{:S(2)}) copy-start(bf16[2,256,256]{2,1,0:T(8,128)(2,1)} %probe.1) | copy-start | bytes 786436
  4.8 0.9 %copy-start.3 = (bf16[1,256,512]{2,1,0:T(8,128)(2,1)S(1)}, bf16[1,256,512]{2,1,0:T(8,128)(2,1)}, u32[]{:S(2)}) copy-start(bf16[1,256,512]{2,1,0:T(8,128)(2,1)} %param.10) | copy-start | bytes 786436
  5.8 0.9 %copy-start.4 = (f32[256,256]{1,0:T(8,128)S(1)}, f32[256,256]{1,0:T(8,128)}, u32[]{:S(2)}) copy-start(f32[256,256]{1,0:T(8,128)} %prop.1) | copy-start | bytes 786436
  6.7 1.0 %copy-start.5 = (bf16[512,512]{1,0:T(8,128)(2,1)S(1)}, bf16[512,512]{1,0:T(8,128)(2,1)}, u32[]{:S(2)}) copy-start(bf16[512,512]{1,0:T(8,128)(2,1)} %constant.5.clone.b_ref) | copy-start | bytes 1572868
  7.8 1.0 %copy-start.6 = (bf16[512,512]{1,0:T(8,128)(2,1)S(1)}, bf16[512,512]{1,0:T(8,128)(2,1)}, u32[]{:S(2)}) copy-start(bf16[512,512]{1,0:T(8,128)(2,1)} %constant.4.clone.a_ref) | copy-start | bytes 1572868

commit v2 on v1

--- a/solution.py
+++ b/solution.py
@@ -56,9 +56,10 @@
     return jnp.concatenate([re.astype(BF16), im.astype(BF16)], axis=0)
 
 
-def kernel(D, N, Pn, pos, a_ref, b_ref, probe, tile, prop, stored, measured,
+def kernel(D, N, Pn, pos, a_hbm, b_hbm, probe_hbm, tile, prop_hbm, stored_hbm, measured_hbm,
            leaving, grad,
-           tiles, nexts, h_ref, waves, rolled, st3, ge_out, ge_in, own, nxt, rim_out, rim_in,
+           a_ref, b_ref, probe, prop, stored, measured, l_sem, m_sem,
+           tiles, nexts, h_ref, waves, rolled, start, st3, ge_out, ge_in, own, nxt, rim_out, rim_in,
            t_send, t_recv, n_send, n_recv, s_send, s_recv, g_send, g_recv, r_send, r_recv):
     n = prop.shape[0]
     slots = st3.shape[0]
@@ -72,6 +73,22 @@
             src_ref=src, dst_ref=dst, send_sem=send, recv_sem=recv,
             device_id=(depth, lat), device_id_type=MESH)
 
+    loads = [
+        pltpu.make_async_copy(source, target, l_sem.at[i])
+        for i, (source, target) in enumerate((
+            (prop_hbm, prop), (probe_hbm, probe), (stored_hbm, stored), (tile, tiles.at[d]),
+            (a_hbm, a_ref), (b_hbm, b_ref)))
+    ]
+    for load in loads:
+        load.start()
+
+    def load_measured(slot):
+        return pltpu.make_async_copy(
+            measured_hbm.at[slot * D + d], measured.at[slot], m_sem.at[slot])
+
+    for slot in range(slots):
+        pl.when(slot * D + d < Pn)(lambda slot=slot: load_measured(slot).start())
+
     barrier = pltpu.get_barrier_semaphore()
     for off in range(1, D):
         pl.semaphore_signal(barrier, inc=1, device_id=(lax.rem(d + off, D), l), device_id_type=MESH)
@@ -89,7 +106,7 @@
         return remote(source, nexts.at[k], n_send.at[k], n_recv.at[k], d, before)
 
     def send_stored(q):
-        return remote(stored.at[q], st3.at[q // D], s_send.at[q], s_recv.at[q // D], q % D, l)
+        return remote(stored_hbm.at[q], st3.at[q // D], s_send.at[q], s_recv.at[q // D], q % D, l)
 
     pass_on(d, tile).start()
     for off in range(1, D):
@@ -100,10 +117,8 @@
         for q in range(Pn):
             if q % D != D - 1:
                 send_stored(q).start()
-            else:
-                st3[q // D] = stored[q]
-
-    tiles[d] = tile[...]
+
+    loads[0].wait()
     c, s = cos_sin(prop[...])
     h_ref[0] = c
     h_ref[1] = s
@@ -133,6 +148,9 @@
         left = one_hot(col == shift(row, r))
         right = one_hot(row == shift(col, c))
         return move(wave, left, right)
+
+    loads[1].wait()
+    loads[2].wait()
 
     @pl.loop(0, Pn)
     def _(q):
@@ -143,13 +161,8 @@
         rolled[q, :n] = re
         rolled[q, n:] = im
 
-    for off in range(1, D):
-        k = lax.rem(d + off, D)
-        recv_tile(k).wait_recv()
-        pass_on(k, tiles.at[k]).start()
-    for off in range(D):
-        k = lax.rem(d + off, D)
-        pass_on(k, tiles.at[k]).wait_recv()
+    for load in loads[3:]:
+        load.wait()
 
     def dft(wave):
         left = jnp.dot(a_ref[...], wave, preferred_element_type=F32).astype(BF16)
@@ -167,11 +180,41 @@
         there = jnp.where(right, nexts[k, :, n:].astype(F32), nexts[k, :, :n].astype(F32))
         return cos_sin(jnp.where(row < r, there, here))
 
-    def through(re, im, t):
-        tr, ti = t
-        fr, fi = dft(pair(re * tr - im * ti, re * ti + im * tr))
+    def through(waves_in, ts):
+        spectra = [
+            dft(pair(re * tr - im * ti, re * ti + im * tr))
+            for (re, im), (tr, ti) in zip(waves_in, ts)
+        ]
         hr, hi = h_ref[0], h_ref[1]
-        return idft(pair(hr * fr - hi * fi, hr * fi + hi * fr))
+        return [idft(pair(hr * fr - hi * fi, hr * fi + hi * fr)) for fr, fi in spectra]
+
+    group = 2 if Pn % 2 == 0 else 1
+
+    def forward(k):
+        @pl.loop(0, Pn // group)
+        def _(i):
+            ps = [i * group + j for j in range(group)]
+            parts = [waves[p].astype(F32) for p in ps]
+            out = through(
+                [(part[:n], part[n:]) for part in parts],
+                [transmission(k, pos[0, p, 0], pos[0, p, 1]) for p in ps])
+            for p, (re, im) in zip(ps, out):
+                waves[p] = pair(re, im)
+
+    @pl.loop(0, D + 1)
+    def _(k):
+        @pl.when((k < D) & (k != d))
+        def _():
+            recv_tile(k).wait_recv()
+            pass_on(k, tiles.at[k]).start()
+
+        @pl.when(k > 0)
+        def _():
+            pass_on(k - 1, tiles.at[k - 1]).wait_recv()
+
+        @pl.when((k > 0) & (k - 1 < d))
+        def _():
+            forward(k - 1)
 
     def send_ge(slot, k, q):
         return remote(ge_out.at[slot, k], ge_in.at[q], g_send.at[slot, k], g_recv.at[q], k, l)
@@ -183,12 +226,23 @@
 
         @pl.when(d != D - 1)
         def _():
-            remote(stored.at[q], st3.at[slot], s_send.at[q], s_recv.at[slot], d, l).wait_recv()
-
-        re, im = roll_in(st3[slot].reshape(2 * n, n), r, c)
-        xr, xi = through(re.astype(F32), im.astype(F32), transmission(D - 1, r, c))
+            remote(stored_hbm.at[q], st3.at[slot], s_send.at[q], s_recv.at[slot], d, l).wait_recv()
+
+        @pl.when(d != D - 1)
+        def _():
+            re, im = roll_in(st3[slot].reshape(2 * n, n), r, c)
+            start[:n] = re
+            start[n:] = im
+
+        @pl.when(d == D - 1)
+        def _():
+            start[...] = rolled[q]
+
+        load_measured(slot).wait()
+        wave = start[...].astype(F32)
+        xr, xi = through([(wave[:n], wave[n:])], [transmission(D - 1, r, c)])[0]
         fr, fi = dft(pair(xr, xi))
-        weight = fr * fr + fi * fi - measured[q]
+        weight = fr * fr + fi * fi - measured[slot]
         gr, gi = idft(pair(weight * fr, weight * fi))
 
         def step(i, g):
@@ -217,16 +271,7 @@
         else:
             pl.when(slot * D + d < Pn)(functools.partial(backward, slot))
 
-    def forward(k, _):
-        def one(p, _):
-            wave = waves[p].astype(F32)
-            re, im = through(wave[:n], wave[n:], transmission(k, pos[0, p, 0], pos[0, p, 1]))
-            waves[p] = pair(re, im)
-            return 0
-
-        return lax.fori_loop(0, Pn, one, 0)
-
-    lax.fori_loop(0, d + 1, forward, 0)
+    forward(d)
 
     @pl.loop(0, Pn)
     def _(p):
@@ -256,9 +301,15 @@
                 target[part, :, :n] = west
                 target[part, :, n:] = east
 
-    rim_out[...] = nxt[...].astype(BF16)
-    rim = remote(rim_out, rim_in, r_send, r_recv, d, after)
-    rim.start()
+    rims = []
+    for part in range(2):
+        for half in range(2):
+            at = (part, pl.ds(half * n // 2, n // 2))
+            rim_out[at] = nxt[at].astype(BF16)
+            i = 2 * part + half
+            rims.append((at, remote(
+                rim_out.at[at], rim_in.at[at], r_send.at[i], r_recv.at[i], d, after)))
+            rims[-1][1].start()
 
     for off in range(1, D):
         send_tile(lax.rem(d + off, D)).wait_send()
@@ -277,8 +328,9 @@
                 send_ge(slot, lax.rem(d + off, D), slot * D + d).wait_send()
         pl.when(slot * D + d < Pn)(drain)
 
-    rim.wait()
-    grad[...] = own[...] + rim_in[...].astype(F32)
+    for at, rim in rims:
+        rim.wait()
+        grad[at] = own[at] + rim_in[at].astype(F32)
 
 
 def body(probe, positions, object_phase, propagator, stored, measured):
@@ -291,6 +343,7 @@
     slots = -(-Pn // D)
     ahead, back = tables(n)
     vmem = pl.BlockSpec(memory_space=pltpu.VMEM)
+    hbm = pl.BlockSpec(memory_space=pl.ANY)
     smem = pl.BlockSpec(memory_space=pltpu.SMEM)
     dma = pltpu.SemaphoreType.DMA
     leaving, grad = pl.pallas_call(
@@ -299,14 +352,22 @@
             jax.ShapeDtypeStruct((Pn, 2, n, n), BF16),
             jax.ShapeDtypeStruct((2, n, 2 * n), F32),
         ),
-        in_specs=[smem] + [vmem] * 7,
+        in_specs=[smem] + [hbm] * 7,
         out_specs=(vmem, vmem),
         scratch_shapes=[
+            pltpu.VMEM((2 * n, 2 * n), BF16),
+            pltpu.VMEM((2 * n, 2 * n), BF16),
+            pltpu.VMEM((2, n, n), BF16),
+            pltpu.VMEM((n, n), F32),
+            pltpu.VMEM((Pn, 2, n, n), BF16),
+            pltpu.VMEM((slots, n, n), F32),
+            dma((6,)), dma((slots,)),
             pltpu.VMEM((D, n, 2 * n), BF16),
             pltpu.VMEM((D, n, 2 * n), BF16),
             pltpu.VMEM((2, n, n), F32),
             pltpu.VMEM((Pn, 2 * n, n), BF16),
             pltpu.VMEM((Pn, 2 * n, n), BF16),
+            pltpu.VMEM((2 * n, n), BF16),
             pltpu.VMEM((slots, 2, n, n), BF16),
             pltpu.VMEM((slots, D, 2 * n, n), BF16),
             pltpu.VMEM((Pn, 2 * n, n), BF16),
@@ -318,10 +379,10 @@
             dma((D,)), dma((D,)),
             dma((Pn,)), dma((slots,)),
             dma((slots, D)), dma((Pn,)),
-            dma, dma,
+            dma((4,)), dma((4,)),
         ],
         compiler_params=pltpu.CompilerParams(
-            collective_id=0, has_side_effects=True, vmem_limit_bytes=48 << 20),
+            collective_id=0, has_side_effects=True, vmem_limit_bytes=60 << 20),
         cost_estimate=pl.CostEstimate(
             flops=(2 * D * Pn + 4 * D) * 16 * n ** 3, bytes_accessed=32 * n * n * 2 * Pn, transcendentals=0),
     )(positions, ahead, back, probe, object_phase[0], propagator, stored[0], measured)

time: 87.6 us -> 71.3 us (0.81)
  the two profiles are of different devices: /device:TPU:6 before, /device:TPU:0 now
where the time goes in v2:
time: 71.3 us; the launch traced here: 71.1 us
  Pallas kernels  65.8 us (92%)
  local copies, waits for them, and re-layouts  4.68 us (7%)
    pallas_call x1, Pallas kernels, body(): pl.pallas_call(functools.partial(kernel, D, N, Pn), out_shape=(jax.ShapeD...  65.8 us
    unnamed x7, local copies, waits for them, and re-layouts  4.68 us

profile of v2, /device:TPU:0, one launch (start us, length us, event | category | flops | bytes accessed | tf_op | source)
XLA Modules:
  0.0 71.1 jit_solution(8762681181104458362)
XLA Ops:
  0.6 0.0 copy-start.1
  0.6 0.7 copy-done.1
  1.3 0.7 copy.10.pos
  2.0 65.8 %shard_map.95 = (bf16[4,2,256,256]{3,2,1,0:T(8,128)(2,1)}, f32[2,256,512]{2,1,0:T(8,128)}) custom-call(s32[2,4,2]{2,1,0:T(4,128)} %copy.10.pos, bf16[512,512]{1,0:T(8,128)(2,1)} %constant.4.clone.a_hbm, bf16[512,512]{1,0:T(8,128)(2,1)} %constant.5.clone.b_hbm, bf16[2,256,256]{2,1,0:T(8,128)(2,1)} %probe_hbm.1, bf16[256,512]{1,0:T(8,128)(2,1)} %bitcast.7, ...), custom_call_target="tpu_custom_call" | custom-call | flops 12884901888 | bytes 16777216 | tf_op jit(solution)/shard_map/pallas_call | solution.py:349
  67.8 0.0 copy-start
  67.8 2.4 %copy.13 = bf16[1,4,2,256,256]{4,3,2,1,0:T(8,128)(2,1)} copy(bf16[1,4,2,256,256]{4,3,2,1,0:T(8,128)(2,1)} %bitcast.5) | data formatting | bytes 2097152
  70.1 0.0 copy-done
  70.1 1.0 %copy.14 = f32[1,2,256,512]{3,2,1,0:T(8,128)} copy(f32[1,2,256,512]{3,2,1,0:T(8,128)S(1)} %bitcast.4) | data formatting | bytes 2097152
Async XLA Ops:
  0.6 0.7 copy-start.1
  67.8 2.4 %copy-start = (f32[2,256,512]{2,1,0:T(8,128)S(1)}, f32[2,256,512]{2,1,0:T(8,128)}, u32[]{:S(2)}) copy-start(f32[2,256,512]{2,1,0:T(8,128)} %get-tuple-element.5) | copy-start | bytes 3145732

commit v3 on v2

--- a/solution.py
+++ b/solution.py
@@ -96,21 +96,28 @@
         pl.semaphore_signal(barrier, inc=1, device_id=(d, other), device_id_type=MESH)
     pl.semaphore_wait(barrier, D + 1)
 
-    def send_tile(j):
-        return remote(tile, tiles.at[d], t_send.at[j], t_recv.at[d], j, l)
-
-    def recv_tile(k):
-        return remote(tile, tiles.at[k], t_send.at[k], t_recv.at[k], d, l)
-
-    def pass_on(k, source):
-        return remote(source, nexts.at[k], n_send.at[k], n_recv.at[k], d, before)
+    half = n // 2
+    spans = [pl.ds(h * half, half) for h in range(2)]
+
+    def send_tile(j, h):
+        return remote(tile.at[spans[h]], tiles.at[d, spans[h]],
+                      t_send.at[j, h], t_recv.at[d, h], j, l)
+
+    def recv_tile(k, h):
+        return remote(tile.at[spans[h]], tiles.at[k, spans[h]],
+                      t_send.at[k, h], t_recv.at[k, h], d, l)
+
+    def pass_on(k, h, source=None):
+        source = tiles.at[k, spans[h]] if source is None else source.at[spans[h]]
+        return remote(source, nexts.at[k, spans[h]], n_send.at[k, h], n_recv.at[k, h], d, before)
 
     def send_stored(q):
         return remote(stored_hbm.at[q], st3.at[q // D], s_send.at[q], s_recv.at[q // D], q % D, l)
 
-    pass_on(d, tile).start()
-    for off in range(1, D):
-        send_tile(lax.rem(d + off, D)).start()
+    for h in range(2):
+        pass_on(d, h, tile).start()
+        for off in range(1, D):
+            send_tile(lax.rem(d + off, D), h).start()
 
     @pl.when(d == D - 1)
     def _():
@@ -201,23 +208,32 @@
             for p, (re, im) in zip(ps, out):
                 waves[p] = pair(re, im)
 
+    @pl.loop(0, D)
+    def _(k):
+        @pl.when(k != d)
+        def _():
+            recv_tile(k, 0).wait_recv()
+            pass_on(k, 0).start()
+
     @pl.loop(0, D + 1)
     def _(k):
         @pl.when((k < D) & (k != d))
         def _():
-            recv_tile(k).wait_recv()
-            pass_on(k, tiles.at[k]).start()
+            recv_tile(k, 1).wait_recv()
+            pass_on(k, 1).start()
 
         @pl.when(k > 0)
         def _():
-            pass_on(k - 1, tiles.at[k - 1]).wait_recv()
+            for h in range(2):
+                pass_on(k - 1, h).wait_recv()
 
         @pl.when((k > 0) & (k - 1 < d))
         def _():
             forward(k - 1)
 
-    def send_ge(slot, k, q):
-        return remote(ge_out.at[slot, k], ge_in.at[q], g_send.at[slot, k], g_recv.at[q], k, l)
+    def send_ge(slot, k, q, h):
+        return remote(ge_out.at[slot, k, h], ge_in.at[q, h],
+                      g_send.at[slot, k, h], g_recv.at[q, h], k, l)
 
     def backward(slot):
         q = slot * D + d
@@ -250,20 +266,27 @@
             fr, fi = dft(g)
             hr, hi = h_ref[0], h_ref[1]
             er, ei = idft(pair(hr * fr + hi * fi, hr * fi - hi * fr))
-            ge_out[slot, k] = pair(er, ei)
+            pieces = [(h, part, value[h * half:(h + 1) * half].astype(BF16))
+                      for h in range(2) for part, value in enumerate((er, ei))]
 
             @pl.when(k == d)
             def _():
-                ge_in[q] = pair(er, ei)
+                for h, part, value in pieces:
+                    ge_in[q, h, part] = value
 
             @pl.when(k != d)
             def _():
-                send_ge(slot, k, q).start()
+                for h, part, value in pieces:
+                    ge_out[slot, k, h, part] = value
+                send_ge(slot, k, q, 0).start()
 
             tr, ti = transmission(k, r, c)
             return pair(tr * er + ti * ei, tr * ei - ti * er)
 
         lax.fori_loop(0, D, step, pair(gr, gi))
+
+        for k in reversed(range(D)):
+            pl.when(k != d)(lambda k=k: send_ge(slot, k, q, 1).start())
 
     for slot in range(slots):
         if (slot + 1) * D <= Pn:
@@ -279,42 +302,45 @@
         leaving[p, 0] = re
         leaving[p, 1] = im
 
-    for q in range(Pn):
-        @pl.when(d != q % D)
-        def _():
-            remote(ge_out.at[0, 0], ge_in.at[q], g_send.at[0, 0], g_recv.at[q], d, l).wait_recv()
-
-        u = rolled[q].astype(F32)
-        g = ge_in[q].astype(F32)
-        ur, ui, gr, gi = u[:n], u[n:], g[:n], g[n:]
-        lower = row < pos[1, q, 0]
-        right = col < pos[1, q, 1]
-        for part, term in enumerate((ur * gr + ui * gi, ur * gi - ui * gr)):
-            here = jnp.where(lower, 0.0, term)
-            there = jnp.where(lower, term, 0.0)
-            for target, value in ((own, here), (nxt, there)):
-                west = jnp.where(right, 0.0, value)
-                east = jnp.where(right, value, 0.0)
-                if q > 0:
-                    west = west + target[part, :, :n]
-                    east = east + target[part, :, n:]
-                target[part, :, :n] = west
-                target[part, :, n:] = east
-
     rims = []
-    for part in range(2):
-        for half in range(2):
-            at = (part, pl.ds(half * n // 2, n // 2))
-            rim_out[at] = nxt[at].astype(BF16)
-            i = 2 * part + half
-            rims.append((at, remote(
-                rim_out.at[at], rim_in.at[at], r_send.at[i], r_recv.at[i], d, after)))
+    for h in range(2):
+        at, lines = spans[h], slice(h * half, (h + 1) * half)
+        for q in range(Pn):
+            @pl.when(d != q % D)
+            def _():
+                remote(ge_out.at[0, 0, h], ge_in.at[q, h],
+                       g_send.at[0, 0, h], g_recv.at[q, h], d, l).wait_recv()
+
+            ur = rolled[q, lines].astype(F32)
+            ui = rolled[q, n + h * half:n + (h + 1) * half].astype(F32)
+            gr, gi = ge_in[q, h, 0].astype(F32), ge_in[q, h, 1].astype(F32)
+            lower = row[lines] < pos[1, q, 0]
+            right = col[lines] < pos[1, q, 1]
+            for part, term in enumerate((ur * gr + ui * gi, ur * gi - ui * gr)):
+                here = jnp.where(lower, 0.0, term)
+                there = jnp.where(lower, term, 0.0)
+                for target, value in ((own, here), (nxt, there)):
+                    west = jnp.where(right, 0.0, value)
+                    east = jnp.where(right, value, 0.0)
+                    if q > 0:
+                        west = west + target[part, lines, :n]
+                        east = east + target[part, lines, n:]
+                    target[part, lines, :n] = west
+                    target[part, lines, n:] = east
+
+        for part in range(2):
+            rim_out[part, lines] = nxt[part, lines].astype(BF16)
+            rims.append(((part, lines), remote(
+                rim_out.at[part, at], rim_in.at[part, at],
+                r_send.at[part, h], r_recv.at[part, h], d, after)))
             rims[-1][1].start()
 
     for off in range(1, D):
-        send_tile(lax.rem(d + off, D)).wait_send()
+        for h in range(2):
+            send_tile(lax.rem(d + off, D), h).wait_send()
     for k in range(D):
-        pass_on(k, tiles.at[k]).wait_send()
+        for h in range(2):
+            pass_on(k, h).wait_send()
 
     @pl.when(d == D - 1)
     def _():
@@ -325,7 +351,8 @@
     for slot in range(slots):
         def drain(slot=slot):
             for off in range(1, D):
-                send_ge(slot, lax.rem(d + off, D), slot * D + d).wait_send()
+                for h in range(2):
+                    send_ge(slot, lax.rem(d + off, D), slot * D + d, h).wait_send()
         pl.when(slot * D + d < Pn)(drain)
 
     for at, rim in rims:
@@ -369,17 +396,17 @@
             pltpu.VMEM((Pn, 2 * n, n), BF16),
             pltpu.VMEM((2 * n, n), BF16),
             pltpu.VMEM((slots, 2, n, n), BF16),
-            pltpu.VMEM((slots, D, 2 * n, n), BF16),
-            pltpu.VMEM((Pn, 2 * n, n), BF16),
+            pltpu.VMEM((slots, D, 2, 2, n // 2, n), BF16),
+            pltpu.VMEM((Pn, 2, 2, n // 2, n), BF16),
             pltpu.VMEM((2, n, 2 * n), F32),
             pltpu.VMEM((2, n, 2 * n), F32),
             pltpu.VMEM((2, n, 2 * n), BF16),
             pltpu.VMEM((2, n, 2 * n), BF16),
-            dma((D,)), dma((D,)),
-            dma((D,)), dma((D,)),
+            dma((D, 2)), dma((D, 2)),
+            dma((D, 2)), dma((D, 2)),
             dma((Pn,)), dma((slots,)),
-            dma((slots, D)), dma((Pn,)),
-            dma((4,)), dma((4,)),
+            dma((slots, D, 2)), dma((Pn, 2)),
+            dma((2, 2)), dma((2, 2)),
         ],
         compiler_params=pltpu.CompilerParams(
             collective_id=0, has_side_effects=True, vmem_limit_bytes=60 << 20),

time: 71.3 us -> 67.8 us (0.951)
  Pallas kernels: 65.8 us -> 62.2 us
    pallas_call x1, Pallas kernels: 65.8 us -> 62.2 us  [body(): pl.pallas_call(functools.partial(kernel, D, N, Pn), out_shape=(jax.ShapeD...]
where the time goes in v3:
time: 67.8 us; the launch traced here: 67.6 us
  Pallas kernels  62.2 us (92%)
  local copies, waits for them, and re-layouts  4.68 us (7%)
    pallas_call x1, Pallas kernels, body(): pl.pallas_call(functools.partial(kernel, D, N, Pn), out_shape=(jax.ShapeD...  62.2 us
    unnamed x7, local copies, waits for them, and re-layouts  4.68 us

profile of v3, /device:TPU:0, one launch (start us, length us, event | category | flops | bytes accessed | tf_op | source)
XLA Modules:
  0.0 67.6 jit_solution(16077893933435446269)
XLA Ops:
  0.6 0.0 copy-start.1
  0.6 0.7 copy-done.1
  1.3 0.7 %copy.10.pos = s32[2,4,2]{2,1,0:T(4,128)} copy(s32[2,4,2]{1,2,0:T(2,128)S(1)} %copy-done.1) | data formatting | bytes 128 | tf_op args[1]
  2.0 62.2 %shard_map.95 = (bf16[4,2,256,256]{3,2,1,0:T(8,128)(2,1)}, f32[2,256,512]{2,1,0:T(8,128)}) custom-call(s32[2,4,2]{2,1,0:T(4,128)} %copy.10.pos, bf16[512,512]{1,0:T(8,128)(2,1)} %constant.4.clone.a_hbm, bf16[512,512]{1,0:T(8,128)(2,1)} %constant.5.clone.b_hbm, bf16[2,256,256]{2,1,0:T(8,128)(2,1)} %probe_hbm.1, bf16[256,512]{1,0:T(8,128)(2,1)} %bitcast.7, ...), custom_call_target="tpu_custom_call" | custom-call | flops 12884901888 | bytes 16777216 | tf_op jit(solution)/shard_map/pallas_call | solution.py:376
  64.2 0.0 copy-start
  64.3 2.4 %copy.13 = bf16[1,4,2,256,256]{4,3,2,1,0:T(8,128)(2,1)} copy(bf16[1,4,2,256,256]{4,3,2,1,0:T(8,128)(2,1)} %bitcast.5) | data formatting | bytes 2097152
  66.6 0.0 copy-done
  66.6 1.0 %copy.14 = f32[1,2,256,512]{3,2,1,0:T(8,128)} copy(f32[1,2,256,512]{3,2,1,0:T(8,128)S(1)} %bitcast.4) | data formatting | bytes 2097152
Async XLA Ops:
  0.6 0.7 %copy-start.1 = (s32[2,4,2]{1,2,0:T(2,128)S(1)}, s32[2,4,2]{1,2,0:T(2,128)}, u32[]{:S(2)}) copy-start(s32[2,4,2]{1,2,0:T(2,128)} %param.9) | copy-start | bytes 196
  64.2 2.4 %copy-start = (f32[2,256,512]{2,1,0:T(8,128)S(1)}, f32[2,256,512]{2,1,0:T(8,128)}, u32[]{:S(2)}) copy-start(f32[2,256,512]{2,1,0:T(8,128)} %get-tuple-element.5) | copy-start | bytes 3145732
